TPU v7x, 32 devices: a whole 2x2x4 slice. The times are simulated.
32 devices in a mesh: wide: 16 (over z, y, core), rep: 2 (over x).
Axes of the slice: x: 2, y: 2, z: 4, core: 2. Of those that a mesh axis runs over, the one named last changes fastest.
Arguments:
- features: bfloat16 [4096, 512], P(('wide', 'rep')), may hold values from -6 to 6
- w_query: bfloat16 [512, 512], replicated, may hold values from -0.25 to 0.25
- w_key: bfloat16 [512, 512], replicated, may hold values from -0.25 to 0.25
- w_out: bfloat16 [512, 512], replicated, may hold values from -0.25 to 0.25
- edge_weight: bfloat16 [16, 2, 6, 128, 128], P('wide', 'rep'), may hold values from -0.23925781 to 0.23925781
- tile_slot: int32 [16, 2, 6], P('wide', 'rep'), may hold values from 0 to 31, as said below
- tile_count: int32 [16, 2], P('wide', 'rep'), may hold values from 1 to 6, as said below
Outputs:
- updated: bfloat16 [4096, 512], P(('wide', 'rep'))
Inputs may be any that keep to these rules, and one draw needn't show every extreme that they name: For each w and r the first tile_count[w, r] entries of tile_slot[w, r] are distinct and ascending; all 6 entries of a list are distinct. `tile_count`: some device has 6 live tiles.
All inputs are finite; a program needn't handle non-finite values.
Results may differ from a plain program's by a relative error of at most 0.014.
Values may be sent and summed in bfloat16 or wider, within the bound.
No kernel may reach another device: no remote copies, remote signals or barrier semaphores. Data moves between devices by JAX's collectives and lax.ppermute only.
A program may use at most 64 MiB of HBM per device.

v0:
```python
import jax
import jax.numpy as jnp
from jax import lax
from jax.experimental import pallas as pl
from jax.experimental.pallas import tpu as pltpu
from jax.sharding import PartitionSpec as P

CORE, NEAR, FAR = 1, 2, 4
NT = (((1,), (1,)), ((), ()))
VMEM = pl.BlockSpec(memory_space=pltpu.VMEM)
SMEM = pl.BlockSpec(memory_space=pltpu.SMEM)
PARAMS = pltpu.CompilerParams(vmem_limit_bytes=40 << 20)


def send(value, k):
    return lax.ppermute(value, "wide", [(w, w ^ k) for w in range(lax.axis_size("wide"))])


def turn_rep(value, turn):
    n_rep = lax.axis_size("rep")
    return lax.ppermute(value, "rep", [(r, (r + turn) % n_rep) for r in range(n_rep)])


def cost(flops):
    return pl.CostEstimate(flops=flops, bytes_accessed=2 << 20, transcendentals=0)


def queries_kernel(n_rep, *refs):
    blocks, (w_query_ref, w_key_ref, query_ref) = refs[:n_rep], refs[n_rep:]
    for part, block_ref in enumerate(blocks):
        query = jnp.dot(
            block_ref[...], w_query_ref[...], preferred_element_type=jnp.float32
        ).astype(jnp.bfloat16)
        query_ref[part] = lax.dot_general(
            query, w_key_ref[...], NT, preferred_element_type=jnp.float32
        ).astype(jnp.bfloat16)


def note_tiles(n_wide, n_rep, list_ref, table_ref):
    wide_pos = lax.axis_index("wide")
    rep_pos = lax.axis_index("rep")
    for k in range(2 * n_wide):
        table_ref[k] = 0

    def note(tile, carry):
        slot = list_ref[1 + tile]
        step = slot // n_rep
        k = wide_pos ^ lax.rem(wide_pos - step + n_wide, n_wide)
        seen = table_ref[n_wide + k]
        table_ref[k] = jnp.where(seen == 0, tile, table_ref[k])
        table_ref[n_wide + k] = seen + 1
        table_ref[2 * n_wide + tile] = lax.rem(slot - step * n_rep - rep_pos + n_rep, n_rep)
        return carry

    lax.fori_loop(0, list_ref[0], note, 0)


def add_tiles(n_wide, factor, pieces, table_ref, weight_ref, query_ref, total, wanted):
    rows = weight_ref.shape[1]
    for block_ref, ks in pieces:
        for i, k in enumerate(ks):

            def one_tile(tile, carry, block_ref=block_ref, i=i):
                part = table_ref[2 * n_wide + tile]
                at = 0 if wanted == "own" else part - 1

                @pl.when((part == 0) if wanted == "own" else (part != 0))
                def _():
                    block = block_ref[i * rows : (i + 1) * rows, :]
                    scores = lax.dot_general(
                        query_ref[part], block, NT, preferred_element_type=jnp.float32
                    )
                    weighted = jnp.tanh(scores * factor) * weight_ref[tile].astype(jnp.float32)
                    total[at] += jnp.dot(
                        weighted.astype(jnp.bfloat16), block, preferred_element_type=jnp.float32
                    )

                return carry

            first = table_ref[k]
            lax.fori_loop(first, first + table_ref[n_wide + k], one_tile, 0)


def early_kernel(layout, n_wide, n_rep, factor, list_ref, weight_ref, query_ref, *rest):
    blocks, (total, table_ref) = rest[: len(layout)], rest[len(layout) :]
    note_tiles(n_wide, n_rep, list_ref, table_ref)
    total[...] = jnp.zeros_like(total)
    pieces = list(zip(blocks, layout))
    add_tiles(n_wide, factor, pieces, table_ref, weight_ref, query_ref, total, "others")


def others_kernel(layout, n_wide, n_rep, factor, list_ref, weight_ref, query_ref, early_ref, *rest):
    blocks, (out_ref, total, table_ref) = rest[: len(layout)], rest[len(layout) :]
    note_tiles(n_wide, n_rep, list_ref, table_ref)
    total[...] = early_ref[...]
    pieces = list(zip(blocks, layout))
    add_tiles(n_wide, factor, pieces, table_ref, weight_ref, query_ref, total, "others")
    out_ref[...] = total[...].astype(jnp.bfloat16)


def own_kernel(layout, n_wide, n_rep, factor, list_ref, weight_ref, query_ref, others_ref, w_key_ref, w_out_ref, features_ref, *rest):
    blocks, (out_ref, both_ref, total, table_ref) = rest[: len(layout)], rest[len(layout) :]
    note_tiles(n_wide, n_rep, list_ref, table_ref)
    total[...] = jnp.zeros_like(total)
    pieces = list(zip(blocks, layout))
    add_tiles(n_wide, factor, pieces, table_ref, weight_ref, query_ref, total, "own")
    both_ref[...] = jnp.dot(
        w_key_ref[...], w_out_ref[...], preferred_element_type=jnp.float32
    ).astype(jnp.bfloat16)
    message = jnp.dot(
        total[0].astype(jnp.bfloat16), w_key_ref[...], preferred_element_type=jnp.float32
    ).astype(jnp.bfloat16)
    out_ref[...] = features_ref[...].astype(jnp.float32) + jnp.dot(
        message, w_out_ref[...], preferred_element_type=jnp.float32
    )


def output_kernel(own_ref, both_ref, *rest):
    *received, out_ref = rest
    mixed = received[0][...]
    if len(received) > 1:
        mixed = sum(ref[...].astype(jnp.float32) for ref in received).astype(jnp.bfloat16)
    updated = own_ref[...] + jnp.dot(mixed, both_ref[...], preferred_element_type=jnp.float32)
    out_ref[...] = updated.astype(jnp.bfloat16)


def on_device(features, w_query, w_key, w_out, edge_weight, tile_slot, tile_count):
    rows, width = features.shape
    n_wide = lax.axis_size("wide")
    n_rep = lax.axis_size("rep")
    factor = 1.0 / float(width) ** 0.5
    weights = edge_weight[0, 0]
    tile_list = jnp.concatenate([tile_count[0], tile_slot[0, 0]])

    held = {0: features, NEAR: send(features, NEAR)}
    relays = []
    far, bit = [0], n_wide // 2
    while bit >= FAR:
        for k in list(far):
            if k and not relays:
                relays = [turn_rep(features, -part) for part in range(1, n_rep)]
            held[k ^ bit] = send(held[k], bit)
            far.append(k ^ bit)
        bit //= 2
    top, end = n_wide // 2, n_wide - FAR
    for k in sorted(far)[1:]:
        value = held[k]
        if k == end:
            value = lax.optimization_barrier((value, *relays))[0]
        held[k ^ NEAR] = send(value, NEAR)

    queries = pl.pallas_call(
        lambda *refs: queries_kernel(n_rep, *refs),
        out_shape=jax.ShapeDtypeStruct((n_rep, rows, width), jnp.bfloat16),
        in_specs=[VMEM] * (n_rep + 2),
        out_specs=VMEM,
        compiler_params=PARAMS,
        cost_estimate=cost(80 * n_rep * rows * width * width),
        name="queries",
    )(features, *relays, w_query, w_key)

    def other_core(ks):
        blocks = [held[k] for k in ks]
        both = jnp.concatenate(blocks, 0) if len(ks) > 1 else blocks[0]
        return send(both, CORE), [k ^ CORE for k in ks]

    groups = [[0, FAR, NEAR], [top, FAR ^ NEAR], [], [end ^ NEAR]]
    groups[2] = [k for k in held if not any(k in group for group in groups)]
    pairs = [other_core(group) for group in groups]
    soon = [0, top, FAR, NEAR, FAR ^ NEAR, end]
    early = [(held[k], [k]) for k in soon] + pairs[:2]
    late = [(held[k], [k]) for k in held if k not in soon] + pairs[2:]

    def call(kernel, pieces, inputs, out_shape, name, scratch=()):
        layout = [ks for _, ks in pieces]
        return pl.pallas_call(
            lambda *refs: kernel(layout, n_wide, n_rep, factor, *refs),
            out_shape=out_shape,
            in_specs=[SMEM] + [VMEM] * (1 + len(inputs) + len(pieces)),
            out_specs=jax.tree.map(lambda _: VMEM, out_shape),
            scratch_shapes=[*scratch, pltpu.SMEM((2 * n_wide + tile_slot.shape[-1],), jnp.int32)],
            compiler_params=PARAMS,
            cost_estimate=cost(240 * rows * rows * width),
            name=name,
        )(tile_list, weights, *inputs, *[block for block, _ in pieces])

    totals = jax.ShapeDtypeStruct((n_rep - 1, rows, width), jnp.float32)
    total = call(early_kernel, early, [queries], totals, "early")
    others = call(
        others_kernel,
        late,
        [queries, total],
        jax.ShapeDtypeStruct((n_rep - 1, rows, width), jnp.bfloat16),
        "others",
        [pltpu.VMEM((n_rep - 1, rows, width), jnp.float32)],
    )
    received = [turn_rep(others[part - 1], part) for part in range(1, n_rep)]
    own, both = call(
        own_kernel,
        early + late,
        [queries, others, w_key, w_out, features],
        (
            jax.ShapeDtypeStruct((rows, width), jnp.float32),
            jax.ShapeDtypeStruct(w_key.shape, jnp.bfloat16),
        ),
        "own",
        [pltpu.VMEM((1, rows, width), jnp.float32)],
    )
    return pl.pallas_call(
        output_kernel,
        out_shape=jax.ShapeDtypeStruct((rows, width), jnp.bfloat16),
        in_specs=[VMEM] * (2 + len(received)),
        out_specs=VMEM,
        compiler_params=PARAMS,
        name="output",
    )(own, both, *received)


def solution(mesh):
    in_specs = (
        P(("wide", "rep"), None),
        P(),
        P(),
        P(),
        P("wide", "rep", None, None, None),
        P("wide", "rep", None),
        P("wide", "rep"),
    )
    out_specs = P(("wide", "rep"), None)
    return jax.shard_map(
        on_device, mesh=mesh, in_specs=in_specs, out_specs=out_specs, check_vma=False
    )
```

profile of v0, /device:TPU:0, one launch (start us, length us, event | category | flops | bytes accessed | tf_op | source)
XLA Modules:
  0.0 31.0 jit_solution(17326200581064830817)
XLA Ops:
  0.0 3.0 %collective-permute-start.2 = (bf16[128,512]{1,0:T(8,128)(2,1)}, bf16[128,512]{1,0:T(8,128)(2,1)S(1)}, u32[]{:S(2)}, u32[]{:S(2)}) collective-permute-start(bf16[128,512]{1,0:T(8,128)(2,1)} %refs_7_.1), channel_id=1, source_target_pairs={{0,8},{2,10},{4,12},{6,14},{8,0},{10,2},{12,4},{14,6},{16,24},{18,... | collective-permute-start | bytes 393224 | tf_op jit(solution)/shard_map/ppermute | solution.py:16
  3.0 2.6 %collective-permute-start.1 = (bf16[128,512]{1,0:T(8,128)(2,1)}, bf16[128,512]{1,0:T(8,128)(2,1)S(1)}, u32[]{:S(2)}, u32[]{:S(2)}) collective-permute-start(bf16[128,512]{1,0:T(8,128)(2,1)} %refs_7_.1), channel_id=1, source_target_pairs={{0,16},{2,18},{4,20},{6,22},{8,24},{10,26},{12,28},{14,30},{16,0},... | collective-permute-start | bytes 393224 | tf_op jit(solution)/shard_map/ppermute | solution.py:16
  5.6 1.5 %collective-permute-start.3 = (bf16[128,512]{1,0:T(8,128)(2,1)}, bf16[128,512]{1,0:T(8,128)(2,1)S(1)}, u32[]{:S(2)}, u32[]{:S(2)}) collective-permute-start(bf16[128,512]{1,0:T(8,128)(2,1)} %refs_7_.1), channel_id=1, source_target_pairs={{0,4},{2,6},{4,0},{6,2},{8,12},{10,14},{12,8},{14,10},{16,20},{18,... | collective-permute-start | bytes 393224 | tf_op jit(solution)/shard_map/ppermute | solution.py:16
  7.1 1.5 %collective-permute-start = (bf16[128,512]{1,0:T(8,128)(2,1)}, bf16[128,512]{1,0:T(8,128)(2,1)S(1)}, u32[]{:S(2)}, u32[]{:S(2)}) collective-permute-start(bf16[128,512]{1,0:T(8,128)(2,1)} %refs_7_.1), channel_id=1, source_target_pairs={{0,1},{1,0},{2,3},{3,2},{4,5},{5,4},{6,7},{7,6},{8,9},{9,8},{10,11... | collective-permute-start | bytes 393224 | tf_op jit(solution)/shard_map/ppermute | solution.py:21
  9.3 1.1 %collective-permute-start.4 = (bf16[128,512]{1,0:T(8,128)(2,1)S(1)}, bf16[128,512]{1,0:T(8,128)(2,1)S(1)}, u32[]{:S(2)}, u32[]{:S(2)}) collective-permute-start(bf16[128,512]{1,0:T(8,128)(2,1)S(1)} %collective-permute-done.2.refs_5_.refs_9_), channel_id=1, source_target_pairs={{0,4},{2,6},{4,0},{6,2},{8,12},{10,14},{12,8},{14,10},{16,20},{18,... | collective-permute-start | bytes 393224 | tf_op jit(solution)/shard_map/ppermute | solution.py:16
  10.4 1.6 %collective-permute-done.1.refs_4_.refs_8_ = bf16[128,512]{1,0:T(8,128)(2,1)S(1)} collective-permute-done((bf16[128,512]{1,0:T(8,128)(2,1)}, bf16[128,512]{1,0:T(8,128)(2,1)S(1)}, u32[]{:S(2)}, u32[]{:S(2)}) %collective-permute-start.1) | collective-permute-done | bytes 131104 | tf_op jit(solution)/shard_map/ppermute | solution.py:16
  12.0 0.4 %collective-permute-start.5 = (bf16[128,512]{1,0:T(8,128)(2,1)S(1)}, bf16[128,512]{1,0:T(8,128)(2,1)S(1)}, u32[]{:S(2)}, u32[]{:S(2)}) collective-permute-start(bf16[128,512]{1,0:T(8,128)(2,1)S(1)} %collective-permute-done.1.refs_4_.refs_8_), channel_id=1, source_target_pairs={{0,8},{2,10},{4,12},{6,14},{8,0},{10,2},{12,4},{14,6},{16,24},{18,... | collective-permute-start | bytes 393224 | tf_op jit(solution)/shard_map/ppermute | solution.py:16
  12.4 0.7 %copy-done.5 = s32[1,1,6]{2,1,0:T(1,128)S(1)} copy-done((s32[1,1,6]{2,1,0:T(1,128)S(1)}, s32[1,1,6]{2,1,0:T(1,128)}, u32[]{:S(2)}) %copy-start.5) | copy-done | bytes 48
  13.1 0.1 pad_add_fusion.refs_0_
  13.1 1.5 %collective-permute-start.8 = (bf16[128,512]{1,0:T(8,128)(2,1)S(1)}, bf16[128,512]{1,0:T(8,128)(2,1)S(1)}, u32[]{:S(2)}, u32[]{:S(2)}) collective-permute-start(bf16[128,512]{1,0:T(8,128)(2,1)S(1)} %collective-permute-done.1.refs_4_.refs_8_), channel_id=1, source_target_pairs={{0,4},{2,6},{4,0},{6,2},{8,12},{10,14},{12,8},{14,10},{16,20},{18,... | collective-permute-start | bytes 393224 | tf_op jit(solution)/shard_map/ppermute | solution.py:16
  14.7 1.0 %pad_maximum_fusion = bf16[384,512]{1,0:T(8,128)(2,1)S(1)} fusion(bf16[128,512]{1,0:T(8,128)(2,1)S(1)} %collective-permute-done.3.refs_6_.refs_10_, bf16[128,512]{1,0:T(8,128)(2,1)S(1)} %collective-permute-done.2.refs_5_.refs_9_, bf16[128,512]{1,0:T(8,128)(2,1)} %refs_7_.1), kind=kLoop, calls=%fused_computation | loop fusion | flops 1179648 | bytes 786432 | tf_op jit(solution)/shard_map/concatenate | solution.py:164
  15.7 0.1 collective-permute-start.6
  15.7 1.2 %collective-permute-done.5.refs_8_.refs_12_ = bf16[128,512]{1,0:T(8,128)(2,1)S(1)} collective-permute-done((bf16[128,512]{1,0:T(8,128)(2,1)S(1)}, bf16[128,512]{1,0:T(8,128)(2,1)S(1)}, u32[]{:S(2)}, u32[]{:S(2)}) %collective-permute-start.5) | collective-permute-done | bytes 131104 | tf_op jit(solution)/shard_map/ppermute | solution.py:16
  16.9 1.5 %collective-permute-start.9 = (bf16[128,512]{1,0:T(8,128)(2,1)S(1)}, bf16[128,512]{1,0:T(8,128)(2,1)S(1)}, u32[]{:S(2)}, u32[]{:S(2)}) collective-permute-start(bf16[128,512]{1,0:T(8,128)(2,1)S(1)} %collective-permute-done.5.refs_8_.refs_12_), channel_id=1, source_target_pairs={{0,4},{2,6},{4,0},{6,2},{8,12},{10,14},{12,8},{14,10},{16,20},{18,... | collective-permute-start | bytes 393224 | tf_op jit(solution)/shard_map/ppermute | solution.py:16
  18.6 0.5 %collective-permute-start.10 = (bf16[256,512]{1,0:T(8,128)(2,1)S(1)}, bf16[256,512]{1,0:T(8,128)(2,1)S(1)}, u32[]{:S(2)}, u32[]{:S(2)}) collective-permute-start(bf16[256,512]{1,0:T(8,128)(2,1)S(1)} %pad_maximum_fusion.2), channel_id=1, source_target_pairs={{0,2},{2,0},{4,6},{6,4},{8,10},{10,8},{12,14},{14,12},{16,18},{18,... | collective-permute-start | bytes 786440 | tf_op jit(solution)/shard_map/ppermute | solution.py:16
  19.2 0.2 copy-done
  19.4 0.7 %queries.1.refs_2_ = bf16[2,128,512]{2,1,0:T(8,128)(2,1)S(1)} custom-call(bf16[128,512]{1,0:T(8,128)(2,1)S(1)} %copy-done, bf16[128,512]{1,0:T(8,128)(2,1)S(1)} %collective-permute-done.refs_1_, bf16[512,512]{1,0:T(8,128)(2,1)S(1)} %copy-done.1, bf16[512,512]{1,0:T(8,128)(2,1)S(1)} %copy-done.2), custom_call_target="tpu_custom_call" | custom-call | flops 5368709120 | bytes 2097152 | tf_op jit(solution)/shard_map/queries/pallas_call | solution.py:152
  20.1 1.8 %collective-permute-done.9.refs_5_.refs_16_ = bf16[128,512]{1,0:T(8,128)(2,1)S(1)} collective-permute-done((bf16[128,512]{1,0:T(8,128)(2,1)S(1)}, bf16[128,512]{1,0:T(8,128)(2,1)S(1)}, u32[]{:S(2)}, u32[]{:S(2)}) %collective-permute-start.9) | collective-permute-done | bytes 131104 | tf_op jit(solution)/shard_map/ppermute | solution.py:16
  21.9 2.3 %early.1.refs_3_ = f32[1,128,512]{2,1,0:T(8,128)S(1)} custom-call(s32[7]{0:T(128)S(1)} %pad_add_fusion.refs_0_, bf16[6,128,128]{2,1,0:T(8,128)(2,1)S(1)} %bitcast.5, bf16[2,128,512]{2,1,0:T(8,128)(2,1)S(1)} %queries.1.refs_2_, bf16[128,512]{1,0:T(8,128)(2,1)S(1)} %copy-done, bf16[128,512]{1,0:T(8,128)(2,1)S(1)} %collective-permute-done.1.refs_4_.refs_8_, ...), custom_call_target="tpu_custom_call" | custom-call | flops 2013265920 | bytes 2097152 | tf_op jit(solution)/shard_map/early/pallas_call | solution.py:176
  24.3 0.8 %others.1.refs_3_ = bf16[1,128,512]{2,1,0:T(8,128)(2,1)S(1)} custom-call(s32[7]{0:T(128)S(1)} %pad_add_fusion.refs_0_, bf16[6,128,128]{2,1,0:T(8,128)(2,1)S(1)} %bitcast.6, bf16[2,128,512]{2,1,0:T(8,128)(2,1)S(1)} %queries.1.refs_2_, f32[1,128,512]{2,1,0:T(8,128)S(1)} %early.1.refs_3_, bf16[128,512]{1,0:T(8,128)(2,1)S(1)} %collective-permute-done.8.refs_4_.refs_15_, ...), custom_call_target="tpu_custom_call" | custom-call | flops 2013265920 | bytes 2097152 | tf_op jit(solution)/shard_map/others/pallas_call | solution.py:176
  25.1 0.8 %collective-permute-start.12 = (bf16[128,512]{1,0:T(8,128)(2,1)S(1)}, bf16[128,512]{1,0:T(8,128)(2,1)S(1)}, u32[]{:S(2)}, u32[]{:S(2)}) collective-permute-start(bf16[128,512]{1,0:T(8,128)(2,1)S(1)} %bitcast.8), channel_id=1, source_target_pairs={{0,1},{1,0},{2,3},{3,2},{4,5},{5,4},{6,7},{7,6},{8,9},{9,8},{10,11... | collective-permute-start | bytes 393224 | tf_op jit(solution)/shard_map/ppermute | solution.py:21
  25.9 2.3 %own.1 = (f32[128,512]{1,0:T(8,128)S(1)}, bf16[512,512]{1,0:T(8,128)(2,1)S(1)}) custom-call(s32[7]{0:T(128)S(1)} %pad_add_fusion.refs_0_, bf16[6,128,128]{2,1,0:T(8,128)(2,1)S(1)} %bitcast.7, bf16[2,128,512]{2,1,0:T(8,128)(2,1)S(1)} %queries.1.refs_2_, bf16[1,128,512]{2,1,0:T(8,128)(2,1)S(1)} %others.1.refs_3_, bf16[512,512]{1,0:T(8,128)(2,1)S(1)} %copy-done.2, ...), custom_call_target="tpu_custom_call" | custom-call | flops 2013265920 | bytes 2097152 | tf_op jit(solution)/shard_map/own/pallas_call | solution.py:176
  28.2 1.9 %collective-permute-done.12.rest_0_ = bf16[128,512]{1,0:T(8,128)(2,1)S(1)} collective-permute-done((bf16[128,512]{1,0:T(8,128)(2,1)S(1)}, bf16[128,512]{1,0:T(8,128)(2,1)S(1)}, u32[]{:S(2)}, u32[]{:S(2)}) %collective-permute-start.12) | collective-permute-done | bytes 131104 | tf_op jit(solution)/shard_map/ppermute | solution.py:21
  30.1 0.9 %output.1 = bf16[128,512]{1,0:T(8,128)(2,1)} custom-call(f32[128,512]{1,0:T(8,128)S(1)} %get-tuple-element.9.own_ref, bf16[512,512]{1,0:T(8,128)(2,1)S(1)} %get-tuple-element.10.both_ref, bf16[128,512]{1,0:T(8,128)(2,1)S(1)} %collective-permute-done.12.rest_0_), custom_call_target="tpu_custom_call" | custom-call | tf_op jit(solution)/shard_map/output/pallas_call | solution.py:209
  (23 shorter events, 0.2 us)
Async XLA Ops:
  0.0 9.3 %collective-permute-start.2 = (bf16[128,512]{1,0:T(8,128)(2,1)}, bf16[128,512]{1,0:T(8,128)(2,1)S(1)}, u32[]{:S(2)}, u32[]{:S(2)}) collective-permute-start(bf16[128,512]{1,0:T(8,128)(2,1)} %refs_7_.1), channel_id=1, source_target_pairs={{0,8},{2,10},{4,12},{6,14},{8,0},{10,2},{12,4},{14,6},{16,24},{18,... | collective-permute-start | bytes 393224 | tf_op jit(solution)/shard_map/ppermute | solution.py:16
  3.0 8.9 %collective-permute-start.1 = (bf16[128,512]{1,0:T(8,128)(2,1)}, bf16[128,512]{1,0:T(8,128)(2,1)S(1)}, u32[]{:S(2)}, u32[]{:S(2)}) collective-permute-start(bf16[128,512]{1,0:T(8,128)(2,1)} %refs_7_.1), channel_id=1, source_target_pairs={{0,16},{2,18},{4,20},{6,22},{8,24},{10,26},{12,28},{14,30},{16,0},... | collective-permute-start | bytes 393224 | tf_op jit(solution)/shard_map/ppermute | solution.py:16
  5.6 9.0 %collective-permute-start.3 = (bf16[128,512]{1,0:T(8,128)(2,1)}, bf16[128,512]{1,0:T(8,128)(2,1)S(1)}, u32[]{:S(2)}, u32[]{:S(2)}) collective-permute-start(bf16[128,512]{1,0:T(8,128)(2,1)} %refs_7_.1), channel_id=1, source_target_pairs={{0,4},{2,6},{4,0},{6,2},{8,12},{10,14},{12,8},{14,10},{16,20},{18,... | collective-permute-start | bytes 393224 | tf_op jit(solution)/shard_map/ppermute | solution.py:16
  7.1 8.6 %collective-permute-start = (bf16[128,512]{1,0:T(8,128)(2,1)}, bf16[128,512]{1,0:T(8,128)(2,1)S(1)}, u32[]{:S(2)}, u32[]{:S(2)}) collective-permute-start(bf16[128,512]{1,0:T(8,128)(2,1)} %refs_7_.1), channel_id=1, source_target_pairs={{0,1},{1,0},{2,3},{3,2},{4,5},{5,4},{6,7},{7,6},{8,9},{9,8},{10,11... | collective-permute-start | bytes 393224 | tf_op jit(solution)/shard_map/ppermute | solution.py:21
  9.3 9.2 %collective-permute-start.4 = (bf16[128,512]{1,0:T(8,128)(2,1)S(1)}, bf16[128,512]{1,0:T(8,128)(2,1)S(1)}, u32[]{:S(2)}, u32[]{:S(2)}) collective-permute-start(bf16[128,512]{1,0:T(8,128)(2,1)S(1)} %collective-permute-done.2.refs_5_.refs_9_), channel_id=1, source_target_pairs={{0,4},{2,6},{4,0},{6,2},{8,12},{10,14},{12,8},{14,10},{16,20},{18,... | collective-permute-start | bytes 393224 | tf_op jit(solution)/shard_map/ppermute | solution.py:16
  12.0 5.0 %collective-permute-start.5 = (bf16[128,512]{1,0:T(8,128)(2,1)S(1)}, bf16[128,512]{1,0:T(8,128)(2,1)S(1)}, u32[]{:S(2)}, u32[]{:S(2)}) collective-permute-start(bf16[128,512]{1,0:T(8,128)(2,1)S(1)} %collective-permute-done.1.refs_4_.refs_8_), channel_id=1, source_target_pairs={{0,8},{2,10},{4,12},{6,14},{8,0},{10,2},{12,4},{14,6},{16,24},{18,... | collective-permute-start | bytes 393224 | tf_op jit(solution)/shard_map/ppermute | solution.py:16
  12.4 0.7 %copy-start.5 = (s32[1,1,6]{2,1,0:T(1,128)S(1)}, s32[1,1,6]{2,1,0:T(1,128)}, u32[]{:S(2)}) copy-start(s32[1,1,6]{2,1,0:T(1,128)} %param.12) | copy-start | bytes 76
  13.1 5.4 %collective-permute-start.8 = (bf16[128,512]{1,0:T(8,128)(2,1)S(1)}, bf16[128,512]{1,0:T(8,128)(2,1)S(1)}, u32[]{:S(2)}, u32[]{:S(2)}) collective-permute-start(bf16[128,512]{1,0:T(8,128)(2,1)S(1)} %collective-permute-done.1.refs_4_.refs_8_), channel_id=1, source_target_pairs={{0,4},{2,6},{4,0},{6,2},{8,12},{10,14},{12,8},{14,10},{16,20},{18,... | collective-permute-start | bytes 393224 | tf_op jit(solution)/shard_map/ppermute | solution.py:16
  14.7 4.5 %copy-start.2 = (bf16[512,512]{1,0:T(8,128)(2,1)S(1)}, bf16[512,512]{1,0:T(8,128)(2,1)}, u32[]{:S(2)}) copy-start(bf16[512,512]{1,0:T(8,128)(2,1)} %refs_4_.1) | copy-start | bytes 1572868
  15.6 3.5 %copy-start.1 = (bf16[512,512]{1,0:T(8,128)(2,1)S(1)}, bf16[512,512]{1,0:T(8,128)(2,1)}, u32[]{:S(2)}) copy-start(bf16[512,512]{1,0:T(8,128)(2,1)} %refs_2_.1) | copy-start | bytes 1572868
  15.7 6.3 %collective-permute-start.6 = (bf16[384,512]{1,0:T(8,128)(2,1)S(1)}, bf16[384,512]{1,0:T(8,128)(2,1)S(1)}, u32[]{:S(2)}, u32[]{:S(2)}) collective-permute-start(bf16[384,512]{1,0:T(8,128)(2,1)S(1)} %pad_maximum_fusion), channel_id=1, source_target_pairs={{0,2},{2,0},{4,6},{6,4},{8,10},{10,8},{12,14},{14,12},{16,18},{18,... | collective-permute-start | bytes 1179656 | tf_op jit(solution)/shard_map/ppermute | solution.py:16
  16.9 5.0 %collective-permute-start.9 = (bf16[128,512]{1,0:T(8,128)(2,1)S(1)}, bf16[128,512]{1,0:T(8,128)(2,1)S(1)}, u32[]{:S(2)}, u32[]{:S(2)}) collective-permute-start(bf16[128,512]{1,0:T(8,128)(2,1)S(1)} %collective-permute-done.5.refs_8_.refs_12_), channel_id=1, source_target_pairs={{0,4},{2,6},{4,0},{6,2},{8,12},{10,14},{12,8},{14,10},{16,20},{18,... | collective-permute-start | bytes 393224 | tf_op jit(solution)/shard_map/ppermute | solution.py:16
  18.5 0.9 %copy-start = (bf16[128,512]{1,0:T(8,128)(2,1)S(1)}, bf16[128,512]{1,0:T(8,128)(2,1)}, u32[]{:S(2)}) copy-start(bf16[128,512]{1,0:T(8,128)(2,1)} %refs_7_.1) | copy-start | bytes 393220
  18.5 3.4 %collective-permute-start.7 = (bf16[256,512]{1,0:T(8,128)(2,1)S(1)}, bf16[256,512]{1,0:T(8,128)(2,1)S(1)}, u32[]{:S(2)}, u32[]{:S(2)}) collective-permute-start(bf16[256,512]{1,0:T(8,128)(2,1)S(1)} %pad_maximum_fusion.1), channel_id=1, source_target_pairs={{0,2},{2,0},{4,6},{6,4},{8,10},{10,8},{12,14},{14,12},{16,18},{18,... | collective-permute-start | bytes 786440 | tf_op jit(solution)/shard_map/ppermute | solution.py:16
  18.6 3.3 %copy-start.4 = (bf16[1,1,6,128,128]{4,3,2,1,0:T(8,128)(2,1)S(1)}, bf16[1,1,6,128,128]{4,3,2,1,0:T(8,128)(2,1)}, u32[]{:S(2)}) copy-start(bf16[1,1,6,128,128]{4,3,2,1,0:T(8,128)(2,1)} %param.11) | copy-start | bytes 589828
  18.6 5.7 %collective-permute-start.10 = (bf16[256,512]{1,0:T(8,128)(2,1)S(1)}, bf16[256,512]{1,0:T(8,128)(2,1)S(1)}, u32[]{:S(2)}, u32[]{:S(2)}) collective-permute-start(bf16[256,512]{1,0:T(8,128)(2,1)S(1)} %pad_maximum_fusion.2), channel_id=1, source_target_pairs={{0,2},{2,0},{4,6},{6,4},{8,10},{10,8},{12,14},{14,12},{16,18},{18,... | collective-permute-start | bytes 786440 | tf_op jit(solution)/shard_map/ppermute | solution.py:16
  21.9 2.4 %collective-permute-start.11 = (bf16[128,512]{1,0:T(8,128)(2,1)S(1)}, bf16[128,512]{1,0:T(8,128)(2,1)S(1)}, u32[]{:S(2)}, u32[]{:S(2)}) collective-permute-start(bf16[128,512]{1,0:T(8,128)(2,1)S(1)} %collective-permute-done.9.refs_5_.refs_16_), channel_id=1, source_target_pairs={{0,2},{2,0},{4,6},{6,4},{8,10},{10,8},{12,14},{14,12},{16,18},{18,... | collective-permute-start | bytes 393224 | tf_op jit(solution)/shard_map/ppermute | solution.py:16
  24.3 1.6 %copy-start.3 = (bf16[512,512]{1,0:T(8,128)(2,1)S(1)}, bf16[512,512]{1,0:T(8,128)(2,1)}, u32[]{:S(2)}) copy-start(bf16[512,512]{1,0:T(8,128)(2,1)} %refs_5_.1) | copy-start | bytes 1572868
  25.1 5.0 %collective-permute-start.12 = (bf16[128,512]{1,0:T(8,128)(2,1)S(1)}, bf16[128,512]{1,0:T(8,128)(2,1)S(1)}, u32[]{:S(2)}, u32[]{:S(2)}) collective-permute-start(bf16[128,512]{1,0:T(8,128)(2,1)S(1)} %bitcast.8), channel_id=1, source_target_pairs={{0,1},{1,0},{2,3},{3,2},{4,5},{5,4},{6,7},{7,6},{8,9},{9,8},{10,11... | collective-permute-start | bytes 393224 | tf_op jit(solution)/shard_map/ppermute | solution.py:21
where the time goes:
time: 31.1 us; the launch traced here: 31 us
  starting transfers between devices  14.7 us (47%)
  Pallas kernels  7.04 us (23%)
  waiting for transfers between devices  6.47 us (21%)
  other arithmetic  1.1 us (4%)
  local copies, waits for them, and re-layouts  0.89 us (3%)
  between operations  0.81 us (3%)
    ppermute x11, starting transfers between devices, send(): lax.ppermute(value, 'wide', [(w, w ^ k) for w in range(lax.axis_size('wid...  12.4 us
    pallas_call x3, Pallas kernels, call(): pl.pallas_call(lambda *refs: kernel(layout, n_wide, n_rep, factor, *refs)...  5.41 us
    ppermute x11, waiting for transfers between devices, send(): lax.ppermute(value, 'wide', [(w, w ^ k) for w in range(lax.axis_size('wid...  4.55 us
    ppermute x2, starting transfers between devices, turn_rep(): lax.ppermute(value, 'rep', [(r, (r + turn) % n_rep) for r in range(n_rep)])  2.28 us
    ppermute x2, waiting for transfers between devices, turn_rep(): lax.ppermute(value, 'rep', [(r, (r + turn) % n_rep) for r in range(n_rep)])  1.92 us
    concatenate x3, other arithmetic, other_core(): both = jnp.concatenate(blocks, 0) if len(ks) > 1 else blocks[0]  1.03 us
    pallas_call x1, Pallas kernels, on_device(): pl.pallas_call(output_kernel, out_shape=jax.ShapeDtypeStruct((rows, width...  0.9 us
    unnamed x12, local copies, waits for them, and re-layouts  0.89 us
  transfers between devices with their start and end apart: 13, of which 4 were waited for; matrix products, arithmetic and copies ran while one was open for 4% of the time, Pallas kernels for 17%

commit v1 on v0

--- a/solution.py
+++ b/solution.py
@@ -138,7 +138,8 @@
     while bit >= FAR:
         for k in list(far):
             if k and not relays:
-                relays = [turn_rep(features, -part) for part in range(1, n_rep)]
+                ready = lax.optimization_barrier((features, tile_list))[0]
+                relays = [turn_rep(ready, -part) for part in range(1, n_rep)]
             held[k ^ bit] = send(held[k], bit)
             far.append(k ^ bit)
         bit //= 2

time: 31.1 us -> 31.5 us (1.013); the launches traced: 31 us -> 31.7 us
  waiting for transfers between devices: 6.47 us -> 8.78 us
  Pallas kernels: 7.04 us -> 4.78 us
  starting transfers between devices: 14.7 us -> 15.6 us
    pallas_call x3, Pallas kernels: 5.41 us -> 3.15 us  [call(): pl.pallas_call(lambda *refs: kernel(layout, n_wide, n_rep, factor, *refs)...]
    ppermute x11, waiting for transfers between devices: 4.55 us -> 6.33 us  [send(): lax.ppermute(value, 'wide', [(w, w ^ k) for w in range(lax.axis_size('wid...]
    ppermute x2, starting transfers between devices: 2.28 us -> 3.91 us  [turn_rep(): lax.ppermute(value, 'rep', [(r, (r + turn) % n_rep) for r in range(n_rep)])]
    ppermute x11, starting transfers between devices: 12.4 us -> 11.7 us  [send(): lax.ppermute(value, 'wide', [(w, w ^ k) for w in range(lax.axis_size('wid...]
    ppermute x2, waiting for transfers between devices: 1.92 us -> 2.45 us  [turn_rep(): lax.ppermute(value, 'rep', [(r, (r + turn) % n_rep) for r in range(n_rep)])]
  transfers between devices with their start and end apart: 13 -> 13, of which waited for: 4 -> 7; matrix products, arithmetic and copies ran while one was open for 4% -> 3% of each run, Pallas kernels for 17% -> 10%
where the time goes in v1:
time: 31.5 us; the launch traced here: 31.7 us
  starting transfers between devices  15.6 us (50%)
  waiting for transfers between devices  8.78 us (28%)
  Pallas kernels  4.78 us (15%)
  other arithmetic  1.1 us (3%)
  between operations  0.81 us (3%)
  local copies, waits for them, and re-layouts  0.68 us (2%)
    ppermute x11, starting transfers between devices, send(): lax.ppermute(value, 'wide', [(w, w ^ k) for w in range(lax.axis_size('wid...  11.7 us
    ppermute x11, waiting for transfers between devices, send(): lax.ppermute(value, 'wide', [(w, w ^ k) for w in range(lax.axis_size('wid...  6.33 us
    ppermute x2, starting transfers between devices, turn_rep(): lax.ppermute(value, 'rep', [(r, (r + turn) % n_rep) for r in range(n_rep)])  3.91 us
    pallas_call x3, Pallas kernels, call(): pl.pallas_call(lambda *refs: kernel(layout, n_wide, n_rep, factor, *refs)...  3.15 us
    ppermute x2, waiting for transfers between devices, turn_rep(): lax.ppermute(value, 'rep', [(r, (r + turn) % n_rep) for r in range(n_rep)])  2.45 us
    concatenate x3, other arithmetic, other_core(): both = jnp.concatenate(blocks, 0) if len(ks) > 1 else blocks[0]  1.02 us
    pallas_call x1, Pallas kernels, on_device(): pl.pallas_call(output_kernel, out_shape=jax.ShapeDtypeStruct((rows, width...  0.9 us
    pallas_call x1, Pallas kernels, on_device(): pl.pallas_call(lambda *refs: queries_kernel(n_rep, *refs), out_shape=jax....  0.74 us
  transfers between devices with their start and end apart: 13, of which 7 were waited for; matrix products, arithmetic and copies ran while one was open for 3% of the time, Pallas kernels for 10%

profile of v1, /device:TPU:0, one launch (start us, length us, event | category | flops | bytes accessed | tf_op | source)
XLA Modules:
  0.0 31.7 jit_solution(11161352596058444089)
XLA Ops:
  0.0 4.0 %collective-permute-start.1 = (bf16[128,512]{1,0:T(8,128)(2,1)}, bf16[128,512]{1,0:T(8,128)(2,1)S(1)}, u32[]{:S(2)}, u32[]{:S(2)}) collective-permute-start(bf16[128,512]{1,0:T(8,128)(2,1)} %refs_7_.1), channel_id=1, source_target_pairs={{0,16},{2,18},{4,20},{6,22},{8,24},{10,26},{12,28},{14,30},{16,0},... | collective-permute-start | bytes 393224 | tf_op jit(solution)/shard_map/ppermute | solution.py:16
  4.0 1.6 %collective-permute-start.2 = (bf16[128,512]{1,0:T(8,128)(2,1)}, bf16[128,512]{1,0:T(8,128)(2,1)S(1)}, u32[]{:S(2)}, u32[]{:S(2)}) collective-permute-start(bf16[128,512]{1,0:T(8,128)(2,1)} %refs_7_.1), channel_id=1, source_target_pairs={{0,8},{2,10},{4,12},{6,14},{8,0},{10,2},{12,4},{14,6},{16,24},{18,... | collective-permute-start | bytes 393224 | tf_op jit(solution)/shard_map/ppermute | solution.py:16
  5.6 1.5 %collective-permute-start.3 = (bf16[128,512]{1,0:T(8,128)(2,1)}, bf16[128,512]{1,0:T(8,128)(2,1)S(1)}, u32[]{:S(2)}, u32[]{:S(2)}) collective-permute-start(bf16[128,512]{1,0:T(8,128)(2,1)} %refs_7_.1), channel_id=1, source_target_pairs={{0,4},{2,6},{4,0},{6,2},{8,12},{10,14},{12,8},{14,10},{16,20},{18,... | collective-permute-start | bytes 393224 | tf_op jit(solution)/shard_map/ppermute | solution.py:16
  7.8 0.6 %copy-done.5 = s32[1,1,6]{2,1,0:T(1,128)S(1)} copy-done((s32[1,1,6]{2,1,0:T(1,128)S(1)}, s32[1,1,6]{2,1,0:T(1,128)}, u32[]{:S(2)}) %copy-start.5) | copy-done | bytes 48
  8.4 0.1 pad_add_fusion.refs_0_
  8.5 1.5 %collective-permute-start = (bf16[128,512]{1,0:T(8,128)(2,1)}, bf16[128,512]{1,0:T(8,128)(2,1)S(1)}, u32[]{:S(2)}, u32[]{:S(2)}) collective-permute-start(bf16[128,512]{1,0:T(8,128)(2,1)} %refs_7_.1), channel_id=1, source_target_pairs={{0,1},{1,0},{2,3},{3,2},{4,5},{5,4},{6,7},{7,6},{8,9},{9,8},{10,11... | collective-permute-start | bytes 393224 | tf_op jit(solution)/shard_map/ppermute | solution.py:21
  10.0 0.6 %collective-permute-done.1.refs_4_.refs_8_ = bf16[128,512]{1,0:T(8,128)(2,1)S(1)} collective-permute-done((bf16[128,512]{1,0:T(8,128)(2,1)}, bf16[128,512]{1,0:T(8,128)(2,1)S(1)}, u32[]{:S(2)}, u32[]{:S(2)}) %collective-permute-start.1) | collective-permute-done | bytes 131104 | tf_op jit(solution)/shard_map/ppermute | solution.py:16
  10.7 0.7 %collective-permute-start.5 = (bf16[128,512]{1,0:T(8,128)(2,1)S(1)}, bf16[128,512]{1,0:T(8,128)(2,1)S(1)}, u32[]{:S(2)}, u32[]{:S(2)}) collective-permute-start(bf16[128,512]{1,0:T(8,128)(2,1)S(1)} %collective-permute-done.1.refs_4_.refs_8_), channel_id=1, source_target_pairs={{0,8},{2,10},{4,12},{6,14},{8,0},{10,2},{12,4},{14,6},{16,24},{18,... | collective-permute-start | bytes 393224 | tf_op jit(solution)/shard_map/ppermute | solution.py:16
  11.4 1.5 %collective-permute-start.4 = (bf16[128,512]{1,0:T(8,128)(2,1)S(1)}, bf16[128,512]{1,0:T(8,128)(2,1)S(1)}, u32[]{:S(2)}, u32[]{:S(2)}) collective-permute-start(bf16[128,512]{1,0:T(8,128)(2,1)S(1)} %collective-permute-done.2.refs_5_.refs_9_), channel_id=1, source_target_pairs={{0,4},{2,6},{4,0},{6,2},{8,12},{10,14},{12,8},{14,10},{16,20},{18,... | collective-permute-start | bytes 393224 | tf_op jit(solution)/shard_map/ppermute | solution.py:16
  12.9 0.5 %collective-permute-start.8 = (bf16[128,512]{1,0:T(8,128)(2,1)S(1)}, bf16[128,512]{1,0:T(8,128)(2,1)S(1)}, u32[]{:S(2)}, u32[]{:S(2)}) collective-permute-start(bf16[128,512]{1,0:T(8,128)(2,1)S(1)} %collective-permute-done.1.refs_4_.refs_8_), channel_id=1, source_target_pairs={{0,4},{2,6},{4,0},{6,2},{8,12},{10,14},{12,8},{14,10},{16,20},{18,... | collective-permute-start | bytes 393224 | tf_op jit(solution)/shard_map/ppermute | solution.py:16
  13.4 1.0 %pad_maximum_fusion = bf16[384,512]{1,0:T(8,128)(2,1)S(1)} fusion(bf16[128,512]{1,0:T(8,128)(2,1)S(1)} %collective-permute-done.3.refs_6_.refs_10_, bf16[128,512]{1,0:T(8,128)(2,1)S(1)} %collective-permute-done.2.refs_5_.refs_9_, bf16[128,512]{1,0:T(8,128)(2,1)} %refs_7_.1), kind=kLoop, calls=%fused_computation | loop fusion | flops 1179648 | bytes 786432 | tf_op jit(solution)/shard_map/concatenate | solution.py:165
  14.5 1.1 %collective-permute-done.5.refs_8_.refs_12_ = bf16[128,512]{1,0:T(8,128)(2,1)S(1)} collective-permute-done((bf16[128,512]{1,0:T(8,128)(2,1)S(1)}, bf16[128,512]{1,0:T(8,128)(2,1)S(1)}, u32[]{:S(2)}, u32[]{:S(2)}) %collective-permute-start.5) | collective-permute-done | bytes 131104 | tf_op jit(solution)/shard_map/ppermute | solution.py:16
  15.6 1.6 %collective-permute-start.9 = (bf16[128,512]{1,0:T(8,128)(2,1)S(1)}, bf16[128,512]{1,0:T(8,128)(2,1)S(1)}, u32[]{:S(2)}, u32[]{:S(2)}) collective-permute-start(bf16[128,512]{1,0:T(8,128)(2,1)S(1)} %collective-permute-done.5.refs_8_.refs_12_), channel_id=1, source_target_pairs={{0,4},{2,6},{4,0},{6,2},{8,12},{10,14},{12,8},{14,10},{16,20},{18,... | collective-permute-start | bytes 393224 | tf_op jit(solution)/shard_map/ppermute | solution.py:16
  17.2 0.6 %collective-permute-done.4.refs_7_.refs_11_ = bf16[128,512]{1,0:T(8,128)(2,1)S(1)} collective-permute-done((bf16[128,512]{1,0:T(8,128)(2,1)S(1)}, bf16[128,512]{1,0:T(8,128)(2,1)S(1)}, u32[]{:S(2)}, u32[]{:S(2)}) %collective-permute-start.4) | collective-permute-done | bytes 131104 | tf_op jit(solution)/shard_map/ppermute | solution.py:16
  17.9 2.7 %collective-permute-done.8.refs_4_.refs_15_ = bf16[128,512]{1,0:T(8,128)(2,1)S(1)} collective-permute-done((bf16[128,512]{1,0:T(8,128)(2,1)S(1)}, bf16[128,512]{1,0:T(8,128)(2,1)S(1)}, u32[]{:S(2)}, u32[]{:S(2)}) %collective-permute-start.8) | collective-permute-done | bytes 131104 | tf_op jit(solution)/shard_map/ppermute | solution.py:16
  20.7 0.7 %queries.1.refs_2_ = bf16[2,128,512]{2,1,0:T(8,128)(2,1)S(1)} custom-call(bf16[128,512]{1,0:T(8,128)(2,1)S(1)} %copy-done, bf16[128,512]{1,0:T(8,128)(2,1)S(1)} %collective-permute-done.refs_1_, bf16[512,512]{1,0:T(8,128)(2,1)S(1)} %copy-done.1, bf16[512,512]{1,0:T(8,128)(2,1)S(1)} %copy-done.2), custom_call_target="tpu_custom_call" | custom-call | flops 5368709120 | bytes 2097152 | tf_op jit(solution)/shard_map/queries/pallas_call | solution.py:153
  21.5 0.7 %collective-permute-done.9.refs_5_.refs_16_ = bf16[128,512]{1,0:T(8,128)(2,1)S(1)} collective-permute-done((bf16[128,512]{1,0:T(8,128)(2,1)S(1)}, bf16[128,512]{1,0:T(8,128)(2,1)S(1)}, u32[]{:S(2)}, u32[]{:S(2)}) %collective-permute-start.9) | collective-permute-done | bytes 131104 | tf_op jit(solution)/shard_map/ppermute | solution.py:16
  22.2 0.7 %early.1.refs_3_ = f32[1,128,512]{2,1,0:T(8,128)S(1)} custom-call(s32[7]{0:T(128)S(1)} %pad_add_fusion.refs_0_, bf16[6,128,128]{2,1,0:T(8,128)(2,1)S(1)} %bitcast.5, bf16[2,128,512]{2,1,0:T(8,128)(2,1)S(1)} %queries.1.refs_2_, bf16[128,512]{1,0:T(8,128)(2,1)S(1)} %copy-done, bf16[128,512]{1,0:T(8,128)(2,1)S(1)} %collective-permute-done.1.refs_4_.refs_8_, ...), custom_call_target="tpu_custom_call" | custom-call | flops 2013265920 | bytes 2097152 | tf_op jit(solution)/shard_map/early/pallas_call | solution.py:177
  22.9 0.6 %collective-permute-done.11.refs_7_.refs_18_ = bf16[128,512]{1,0:T(8,128)(2,1)S(1)} collective-permute-done((bf16[128,512]{1,0:T(8,128)(2,1)S(1)}, bf16[128,512]{1,0:T(8,128)(2,1)S(1)}, u32[]{:S(2)}, u32[]{:S(2)}) %collective-permute-start.11) | collective-permute-done | bytes 131104 | tf_op jit(solution)/shard_map/ppermute | solution.py:16
  23.5 0.6 %others.1.refs_3_ = bf16[1,128,512]{2,1,0:T(8,128)(2,1)S(1)} custom-call(s32[7]{0:T(128)S(1)} %pad_add_fusion.refs_0_, bf16[6,128,128]{2,1,0:T(8,128)(2,1)S(1)} %bitcast.6, bf16[2,128,512]{2,1,0:T(8,128)(2,1)S(1)} %queries.1.refs_2_, f32[1,128,512]{2,1,0:T(8,128)S(1)} %early.1.refs_3_, bf16[128,512]{1,0:T(8,128)(2,1)S(1)} %collective-permute-done.8.refs_4_.refs_15_, ...), custom_call_target="tpu_custom_call" | custom-call | flops 2013265920 | bytes 2097152 | tf_op jit(solution)/shard_map/others/pallas_call | solution.py:177
  24.2 2.4 %collective-permute-start.12 = (bf16[128,512]{1,0:T(8,128)(2,1)S(1)}, bf16[128,512]{1,0:T(8,128)(2,1)S(1)}, u32[]{:S(2)}, u32[]{:S(2)}) collective-permute-start(bf16[128,512]{1,0:T(8,128)(2,1)S(1)} %bitcast.8), channel_id=1, source_target_pairs={{0,1},{1,0},{2,3},{3,2},{4,5},{5,4},{6,7},{7,6},{8,9},{9,8},{10,11... | collective-permute-start | bytes 393224 | tf_op jit(solution)/shard_map/ppermute | solution.py:21
  26.6 1.8 %own.1 = (f32[128,512]{1,0:T(8,128)S(1)}, bf16[512,512]{1,0:T(8,128)(2,1)S(1)}) custom-call(s32[7]{0:T(128)S(1)} %pad_add_fusion.refs_0_, bf16[6,128,128]{2,1,0:T(8,128)(2,1)S(1)} %bitcast.7, bf16[2,128,512]{2,1,0:T(8,128)(2,1)S(1)} %queries.1.refs_2_, bf16[1,128,512]{2,1,0:T(8,128)(2,1)S(1)} %others.1.refs_3_, bf16[512,512]{1,0:T(8,128)(2,1)S(1)} %copy-done.2, ...), custom_call_target="tpu_custom_call" | custom-call | flops 2013265920 | bytes 2097152 | tf_op jit(solution)/shard_map/own/pallas_call | solution.py:177
  28.4 2.4 %collective-permute-done.12.rest_0_ = bf16[128,512]{1,0:T(8,128)(2,1)S(1)} collective-permute-done((bf16[128,512]{1,0:T(8,128)(2,1)S(1)}, bf16[128,512]{1,0:T(8,128)(2,1)S(1)}, u32[]{:S(2)}, u32[]{:S(2)}) %collective-permute-start.12) | collective-permute-done | bytes 131104 | tf_op jit(solution)/shard_map/ppermute | solution.py:21
  30.8 0.9 %output.1 = bf16[128,512]{1,0:T(8,128)(2,1)} custom-call(f32[128,512]{1,0:T(8,128)S(1)} %get-tuple-element.11.own_ref, bf16[512,512]{1,0:T(8,128)(2,1)S(1)} %get-tuple-element.12.both_ref, bf16[128,512]{1,0:T(8,128)(2,1)S(1)} %collective-permute-done.12.rest_0_), custom_call_target="tpu_custom_call" | custom-call | tf_op jit(solution)/shard_map/output/pallas_call | solution.py:210
  (23 shorter events, 0.3 us)
Async XLA Ops:
  0.0 10.7 %collective-permute-start.1 = (bf16[128,512]{1,0:T(8,128)(2,1)}, bf16[128,512]{1,0:T(8,128)(2,1)S(1)}, u32[]{:S(2)}, u32[]{:S(2)}) collective-permute-start(bf16[128,512]{1,0:T(8,128)(2,1)} %refs_7_.1), channel_id=1, source_target_pairs={{0,16},{2,18},{4,20},{6,22},{8,24},{10,26},{12,28},{14,30},{16,0},... | collective-permute-start | bytes 393224 | tf_op jit(solution)/shard_map/ppermute | solution.py:16
  4.0 7.3 %collective-permute-start.2 = (bf16[128,512]{1,0:T(8,128)(2,1)}, bf16[128,512]{1,0:T(8,128)(2,1)S(1)}, u32[]{:S(2)}, u32[]{:S(2)}) collective-permute-start(bf16[128,512]{1,0:T(8,128)(2,1)} %refs_7_.1), channel_id=1, source_target_pairs={{0,8},{2,10},{4,12},{6,14},{8,0},{10,2},{12,4},{14,6},{16,24},{18,... | collective-permute-start | bytes 393224 | tf_op jit(solution)/shard_map/ppermute | solution.py:16
  5.6 7.8 %collective-permute-start.3 = (bf16[128,512]{1,0:T(8,128)(2,1)}, bf16[128,512]{1,0:T(8,128)(2,1)S(1)}, u32[]{:S(2)}, u32[]{:S(2)}) collective-permute-start(bf16[128,512]{1,0:T(8,128)(2,1)} %refs_7_.1), channel_id=1, source_target_pairs={{0,4},{2,6},{4,0},{6,2},{8,12},{10,14},{12,8},{14,10},{16,20},{18,... | collective-permute-start | bytes 393224 | tf_op jit(solution)/shard_map/ppermute | solution.py:16
  7.8 0.7 %copy-start.5 = (s32[1,1,6]{2,1,0:T(1,128)S(1)}, s32[1,1,6]{2,1,0:T(1,128)}, u32[]{:S(2)}) copy-start(s32[1,1,6]{2,1,0:T(1,128)} %param.12) | copy-start | bytes 76
  8.5 6.0 %collective-permute-start = (bf16[128,512]{1,0:T(8,128)(2,1)}, bf16[128,512]{1,0:T(8,128)(2,1)S(1)}, u32[]{:S(2)}, u32[]{:S(2)}) collective-permute-start(bf16[128,512]{1,0:T(8,128)(2,1)} %refs_7_.1), channel_id=1, source_target_pairs={{0,1},{1,0},{2,3},{3,2},{4,5},{5,4},{6,7},{7,6},{8,9},{9,8},{10,11... | collective-permute-start | bytes 393224 | tf_op jit(solution)/shard_map/ppermute | solution.py:21
  10.7 5.0 %collective-permute-start.5 = (bf16[128,512]{1,0:T(8,128)(2,1)S(1)}, bf16[128,512]{1,0:T(8,128)(2,1)S(1)}, u32[]{:S(2)}, u32[]{:S(2)}) collective-permute-start(bf16[128,512]{1,0:T(8,128)(2,1)S(1)} %collective-permute-done.1.refs_4_.refs_8_), channel_id=1, source_target_pairs={{0,8},{2,10},{4,12},{6,14},{8,0},{10,2},{12,4},{14,6},{16,24},{18,... | collective-permute-start | bytes 393224 | tf_op jit(solution)/shard_map/ppermute | solution.py:16
  11.4 6.4 %collective-permute-start.4 = (bf16[128,512]{1,0:T(8,128)(2,1)S(1)}, bf16[128,512]{1,0:T(8,128)(2,1)S(1)}, u32[]{:S(2)}, u32[]{:S(2)}) collective-permute-start(bf16[128,512]{1,0:T(8,128)(2,1)S(1)} %collective-permute-done.2.refs_5_.refs_9_), channel_id=1, source_target_pairs={{0,4},{2,6},{4,0},{6,2},{8,12},{10,14},{12,8},{14,10},{16,20},{18,... | collective-permute-start | bytes 393224 | tf_op jit(solution)/shard_map/ppermute | solution.py:16
  12.9 7.7 %collective-permute-start.8 = (bf16[128,512]{1,0:T(8,128)(2,1)S(1)}, bf16[128,512]{1,0:T(8,128)(2,1)S(1)}, u32[]{:S(2)}, u32[]{:S(2)}) collective-permute-start(bf16[128,512]{1,0:T(8,128)(2,1)S(1)} %collective-permute-done.1.refs_4_.refs_8_), channel_id=1, source_target_pairs={{0,4},{2,6},{4,0},{6,2},{8,12},{10,14},{12,8},{14,10},{16,20},{18,... | collective-permute-start | bytes 393224 | tf_op jit(solution)/shard_map/ppermute | solution.py:16
  13.4 7.3 %copy-start.2 = (bf16[512,512]{1,0:T(8,128)(2,1)S(1)}, bf16[512,512]{1,0:T(8,128)(2,1)}, u32[]{:S(2)}) copy-start(bf16[512,512]{1,0:T(8,128)(2,1)} %refs_4_.1) | copy-start | bytes 1572868
  14.4 6.3 %copy-start.1 = (bf16[512,512]{1,0:T(8,128)(2,1)S(1)}, bf16[512,512]{1,0:T(8,128)(2,1)}, u32[]{:S(2)}) copy-start(bf16[512,512]{1,0:T(8,128)(2,1)} %refs_2_.1) | copy-start | bytes 1572868
  14.4 7.7 %collective-permute-start.6 = (bf16[384,512]{1,0:T(8,128)(2,1)S(1)}, bf16[384,512]{1,0:T(8,128)(2,1)S(1)}, u32[]{:S(2)}, u32[]{:S(2)}) collective-permute-start(bf16[384,512]{1,0:T(8,128)(2,1)S(1)} %pad_maximum_fusion), channel_id=1, source_target_pairs={{0,2},{2,0},{4,6},{6,4},{8,10},{10,8},{12,14},{14,12},{16,18},{18,... | collective-permute-start | bytes 1179656 | tf_op jit(solution)/shard_map/ppermute | solution.py:16
  15.6 6.5 %collective-permute-start.9 = (bf16[128,512]{1,0:T(8,128)(2,1)S(1)}, bf16[128,512]{1,0:T(8,128)(2,1)S(1)}, u32[]{:S(2)}, u32[]{:S(2)}) collective-permute-start(bf16[128,512]{1,0:T(8,128)(2,1)S(1)} %collective-permute-done.5.refs_8_.refs_12_), channel_id=1, source_target_pairs={{0,4},{2,6},{4,0},{6,2},{8,12},{10,14},{12,8},{14,10},{16,20},{18,... | collective-permute-start | bytes 393224 | tf_op jit(solution)/shard_map/ppermute | solution.py:16
  17.8 2.9 %copy-start = (bf16[128,512]{1,0:T(8,128)(2,1)S(1)}, bf16[128,512]{1,0:T(8,128)(2,1)}, u32[]{:S(2)}) copy-start(bf16[128,512]{1,0:T(8,128)(2,1)} %refs_7_.1) | copy-start | bytes 393220
  17.8 4.3 %collective-permute-start.7 = (bf16[256,512]{1,0:T(8,128)(2,1)S(1)}, bf16[256,512]{1,0:T(8,128)(2,1)S(1)}, u32[]{:S(2)}, u32[]{:S(2)}) collective-permute-start(bf16[256,512]{1,0:T(8,128)(2,1)S(1)} %pad_maximum_fusion.1), channel_id=1, source_target_pairs={{0,2},{2,0},{4,6},{6,4},{8,10},{10,8},{12,14},{14,12},{16,18},{18,... | collective-permute-start | bytes 786440 | tf_op jit(solution)/shard_map/ppermute | solution.py:16
  20.6 1.5 %copy-start.4 = (bf16[1,1,6,128,128]{4,3,2,1,0:T(8,128)(2,1)S(1)}, bf16[1,1,6,128,128]{4,3,2,1,0:T(8,128)(2,1)}, u32[]{:S(2)}) copy-start(bf16[1,1,6,128,128]{4,3,2,1,0:T(8,128)(2,1)} %param.11) | copy-start | bytes 589828
  20.6 2.9 %collective-permute-start.10 = (bf16[256,512]{1,0:T(8,128)(2,1)S(1)}, bf16[256,512]{1,0:T(8,128)(2,1)S(1)}, u32[]{:S(2)}, u32[]{:S(2)}) collective-permute-start(bf16[256,512]{1,0:T(8,128)(2,1)S(1)} %pad_maximum_fusion.2), channel_id=1, source_target_pairs={{0,2},{2,0},{4,6},{6,4},{8,10},{10,8},{12,14},{14,12},{16,18},{18,... | collective-permute-start | bytes 786440 | tf_op jit(solution)/shard_map/ppermute | solution.py:16
  22.1 1.3 %collective-permute-start.11 = (bf16[128,512]{1,0:T(8,128)(2,1)S(1)}, bf16[128,512]{1,0:T(8,128)(2,1)S(1)}, u32[]{:S(2)}, u32[]{:S(2)}) collective-permute-start(bf16[128,512]{1,0:T(8,128)(2,1)S(1)} %collective-permute-done.9.refs_5_.refs_16_), channel_id=1, source_target_pairs={{0,2},{2,0},{4,6},{6,4},{8,10},{10,8},{12,14},{14,12},{16,18},{18,... | collective-permute-start | bytes 393224 | tf_op jit(solution)/shard_map/ppermute | solution.py:16
  22.9 3.7 %copy-start.3 = (bf16[512,512]{1,0:T(8,128)(2,1)S(1)}, bf16[512,512]{1,0:T(8,128)(2,1)}, u32[]{:S(2)}) copy-start(bf16[512,512]{1,0:T(8,128)(2,1)} %refs_5_.1) | copy-start | bytes 1572868
  24.2 6.7 %collective-permute-start.12 = (bf16[128,512]{1,0:T(8,128)(2,1)S(1)}, bf16[128,512]{1,0:T(8,128)(2,1)S(1)}, u32[]{:S(2)}, u32[]{:S(2)}) collective-permute-start(bf16[128,512]{1,0:T(8,128)(2,1)S(1)} %bitcast.8), channel_id=1, source_target_pairs={{0,1},{1,0},{2,3},{3,2},{4,5},{5,4},{6,7},{7,6},{8,9},{9,8},{10,11... | collective-permute-start | bytes 393224 | tf_op jit(solution)/shard_map/ppermute | solution.py:21
